TPU v7x, 32 devices: a whole 2x2x4 slice. The times are simulated.
32 devices in a mesh: group: 2 (over x), pts: 16 (over z, y, core).
Axes of the slice: x: 2, y: 2, z: 4, core: 2. Of those that a mesh axis runs over, the one named last changes fastest.
Arguments:
- coords: int32 [3, 49152], P(None, ('group', 'pts')), parts along dimension 1, may hold values from 0 to 1023
- field: bfloat16 [64, 49152], P(None, ('group', 'pts')), parts along dimension 1, may hold values from -6 to 6
- mode_list: int32 [4096], replicated, may hold values from 0 to 4095, each once
- spec_weight: bfloat16 [2, 4096, 2, 64, 64], P(None, 'pts'), may hold values from -0.5 to 0.5
- bypass_weight: bfloat16 [2, 64, 64], replicated, may hold values from -0.75 to 0.75
- bypass_bias: float32 [2, 64], replicated, may hold values from -3 to 3
Outputs:
- output: bfloat16 [64, 49152], P(None, ('group', 'pts')), parts along dimension 1
There are 2 independent parts, one for each index of `group`. A program takes and returns all parts, laid end to end along the dimension named above; an argument that names none is the same for every part. Nothing has to cross between parts.
Inputs may be any that keep to these rules, and one draw needn't show every extreme that they name: `mode_list`: each of the 4096 mode numbers appears exactly once.
All inputs are finite; a program needn't handle non-finite values.
Results may differ from a plain program's by a relative error of at most 0.0059.
Values may be sent and summed in bfloat16 or wider, within the bound.
No kernel may reach another device: no remote copies, remote signals or barrier semaphores. Data moves between devices by JAX's collectives and lax.ppermute only.
A program may use at most 192 MiB of HBM per device.

v0:
```python
import math
import jax
import jax.numpy as jnp
from jax import lax
from jax.sharding import PartitionSpec as P

KDIM = 16
GRID = 1024
LAYERS = 2
TWO_PI = 2.0 * math.pi


def direct_basis(wave_ids, coords):
    centre = KDIM // 2
    wave_x = wave_ids // (KDIM * KDIM) - centre
    wave_y = wave_ids // KDIM % KDIM - centre
    wave_z = wave_ids % KDIM - centre
    phase_index = (
        wave_x[:, None] * coords[0][None, :]
        + wave_y[:, None] * coords[1][None, :]
        + wave_z[:, None] * coords[2][None, :]
    )
    phase_index = jnp.mod(phase_index, GRID)
    radians = phase_index.astype(jnp.float32) * (TWO_PI / GRID)
    return jnp.concatenate(
        [jnp.cos(radians).astype(jnp.bfloat16), (-jnp.sin(radians)).astype(jnp.bfloat16)], 0
    )


def mix_modes(spectrum, weights):
    width = weights.shape[-1]
    real_in = spectrum[:, :width]
    imag_in = spectrum[:, width:]
    weight_real = weights[:, 0].astype(jnp.float32)
    weight_imag = weights[:, 1].astype(jnp.float32)
    high = lax.Precision.HIGHEST
    real_out = jnp.einsum("kc,kcd->kd", real_in, weight_real, precision=high) - jnp.einsum(
        "kc,kcd->kd", imag_in, weight_imag, precision=high
    )
    imag_out = jnp.einsum("kc,kcd->kd", real_in, weight_imag, precision=high) + jnp.einsum(
        "kc,kcd->kd", imag_in, weight_real, precision=high
    )
    return jnp.concatenate([real_out, imag_out], 1).astype(jnp.bfloat16)


def finish_layer(spectral, field, layer_weight, layer_bias, modes_total):
    direct = lax.dot_general(
        layer_weight, field, (((0,), (0,)), ((), ())), preferred_element_type=jnp.float32
    )
    summed = spectral * (1.0 / math.sqrt(modes_total)) + direct + layer_bias[:, None]
    return jax.nn.gelu(summed, approximate=False).astype(jnp.bfloat16)


def body(coords, field, mode_list, spec_weight, bypass_weight, bypass_bias):
    width = field.shape[0]
    point_count = field.shape[1]
    modes_total = mode_list.shape[0]
    block_size = math.gcd(modes_total, 512)
    block_count = modes_total // block_size
    normaliser = 1.0 / math.sqrt(point_count * lax.axis_size("pts"))

    def basis_for(wave_ids):
        return direct_basis(wave_ids, coords)

    wave_blocks = mode_list.reshape(block_count, block_size)
    blocked = lax.map(basis_for, wave_blocks)
    basis = (
        blocked.reshape(block_count, 2, block_size, point_count)
        .transpose(1, 0, 2, 3)
        .reshape(2 * modes_total, point_count)
    )
    for depth in range(LAYERS):
        current = field
        product = (
            lax.dot_general(
                basis, current, (((1,), (1,)), ((), ())), preferred_element_type=jnp.float32
            )
            * normaliser
        )
        partial_spectrum = jnp.concatenate([product[:modes_total], product[modes_total:]], 1)
        spectrum = lax.psum_scatter(partial_spectrum, "pts", scatter_dimension=0, tiled=True)
        mixed = mix_modes(spectrum, spec_weight[depth])
        gathered = lax.all_gather(mixed, "pts", axis=0, tiled=True)
        stacked = jnp.concatenate([gathered[:, :width], gathered[:, width:]], 0)
        spectral = lax.dot_general(
            stacked, basis, (((0,), (0,)), ((), ())), preferred_element_type=jnp.float32
        )
        field = finish_layer(
            spectral, current, bypass_weight[depth], bypass_bias[depth], modes_total
        )
    return field


def solution(mesh):
    placed = (
        P(None, ("group", "pts")),
        P(None, ("group", "pts")),
        P(),
        P(None, "pts", None, None, None),
        P(),
        P(),
    )
    return jax.shard_map(
        body, mesh=mesh, in_specs=placed, out_specs=P(None, ("group", "pts")), check_vma=False
    )
```

profile of v0, /device:TPU:0, one launch (start us, length us, event | category | flops | bytes accessed | tf_op | source)
XLA Modules:
  0.0 433.3 jit_solution(10487194853132339083)
XLA Ops:
  7.3 131.8 %while.13 = (s32[]{:T(128)}, bf16[8,1024,1536]{2,1,0:T(8,128)(2,1)}, s32[8,512]{1,0:T(8,128)S(1)}, s32[3,1536]{1,0:T(4,128)}, s32[]{:T(128)}) while((s32[]{:T(128)}, bf16[8,1024,1536]{2,1,0:T(8,128)(2,1)}, s32[8,512]{1,0:T(8,128)S(1)}, s32[3,1536]{1,0:T(4,128)}, s32[]{:T(128)}) %tuple.57), condition=%wide.region_1.2_spmd, body=%wide.region_0.1_spmd.sunk | while | flops 22828544 | bytes 9511489 | solution.py:66
  8.2 13.6 %cosine_convert_fusion.2 = (bf16[512,1536]{1,0:T(8,128)(2,1)S(1)}, bf16[512,1536]{1,0:T(8,128)(2,1)S(1)}) fusion(s32[1536]{0:T(1024)S(1)} %get-tuple-element.177, s32[512]{0:T(512)S(1)} %get-tuple-element.178, s32[1536]{0:T(1024)S(1)} %get-tuple-element.179, s32[512]{0:T(512)S(1)} %get-tuple-element.180, s32[1536]{0:T(1024)S(1)} %get-tuple-element.181, ...), kind=kLoop, calls=%fused_computation.9.clone.1 | loop fusion | flops 16515072 | bytes 3170304 | tf_op jit(solution)/shard_map/while/body/eval_jaxpr/convert_element_type | solution.py:26
  21.9 2.0 fusion.71
  24.8 13.6 %cosine_convert_fusion.2 = (bf16[512,1536]{1,0:T(8,128)(2,1)S(1)}, bf16[512,1536]{1,0:T(8,128)(2,1)S(1)}) fusion(s32[1536]{0:T(1024)S(1)} %get-tuple-element.177, s32[512]{0:T(512)S(1)} %get-tuple-element.178, s32[1536]{0:T(1024)S(1)} %get-tuple-element.179, s32[512]{0:T(512)S(1)} %get-tuple-element.180, s32[1536]{0:T(1024)S(1)} %get-tuple-element.181, ...), kind=kLoop, calls=%fused_computation.9.clone.1 | loop fusion | flops 16515072 | bytes 3170304 | tf_op jit(solution)/shard_map/while/body/eval_jaxpr/convert_element_type | solution.py:26
  38.4 2.0 fusion.71
  41.3 13.6 %cosine_convert_fusion.2 = (bf16[512,1536]{1,0:T(8,128)(2,1)S(1)}, bf16[512,1536]{1,0:T(8,128)(2,1)S(1)}) fusion(s32[1536]{0:T(1024)S(1)} %get-tuple-element.177, s32[512]{0:T(512)S(1)} %get-tuple-element.178, s32[1536]{0:T(1024)S(1)} %get-tuple-element.179, s32[512]{0:T(512)S(1)} %get-tuple-element.180, s32[1536]{0:T(1024)S(1)} %get-tuple-element.181, ...), kind=kLoop, calls=%fused_computation.9.clone.1 | loop fusion | flops 16515072 | bytes 3170304 | tf_op jit(solution)/shard_map/while/body/eval_jaxpr/convert_element_type | solution.py:26
  54.9 1.8 fusion.71
  57.7 13.6 %cosine_convert_fusion.2 = (bf16[512,1536]{1,0:T(8,128)(2,1)S(1)}, bf16[512,1536]{1,0:T(8,128)(2,1)S(1)}) fusion(s32[1536]{0:T(1024)S(1)} %get-tuple-element.177, s32[512]{0:T(512)S(1)} %get-tuple-element.178, s32[1536]{0:T(1024)S(1)} %get-tuple-element.179, s32[512]{0:T(512)S(1)} %get-tuple-element.180, s32[1536]{0:T(1024)S(1)} %get-tuple-element.181, ...), kind=kLoop, calls=%fused_computation.9.clone.1 | loop fusion | flops 16515072 | bytes 3170304 | tf_op jit(solution)/shard_map/while/body/eval_jaxpr/convert_element_type | solution.py:26
  71.4 1.9 fusion.71
  74.2 13.6 %cosine_convert_fusion.2 = (bf16[512,1536]{1,0:T(8,128)(2,1)S(1)}, bf16[512,1536]{1,0:T(8,128)(2,1)S(1)}) fusion(s32[1536]{0:T(1024)S(1)} %get-tuple-element.177, s32[512]{0:T(512)S(1)} %get-tuple-element.178, s32[1536]{0:T(1024)S(1)} %get-tuple-element.179, s32[512]{0:T(512)S(1)} %get-tuple-element.180, s32[1536]{0:T(1024)S(1)} %get-tuple-element.181, ...), kind=kLoop, calls=%fused_computation.9.clone.1 | loop fusion | flops 16515072 | bytes 3170304 | tf_op jit(solution)/shard_map/while/body/eval_jaxpr/convert_element_type | solution.py:26
  87.9 1.8 fusion.71
  90.6 13.6 %cosine_convert_fusion.2 = (bf16[512,1536]{1,0:T(8,128)(2,1)S(1)}, bf16[512,1536]{1,0:T(8,128)(2,1)S(1)}) fusion(s32[1536]{0:T(1024)S(1)} %get-tuple-element.177, s32[512]{0:T(512)S(1)} %get-tuple-element.178, s32[1536]{0:T(1024)S(1)} %get-tuple-element.179, s32[512]{0:T(512)S(1)} %get-tuple-element.180, s32[1536]{0:T(1024)S(1)} %get-tuple-element.181, ...), kind=kLoop, calls=%fused_computation.9.clone.1 | loop fusion | flops 16515072 | bytes 3170304 | tf_op jit(solution)/shard_map/while/body/eval_jaxpr/convert_element_type | solution.py:26
  104.3 1.9 fusion.71
  107.1 13.6 %cosine_convert_fusion.2 = (bf16[512,1536]{1,0:T(8,128)(2,1)S(1)}, bf16[512,1536]{1,0:T(8,128)(2,1)S(1)}) fusion(s32[1536]{0:T(1024)S(1)} %get-tuple-element.177, s32[512]{0:T(512)S(1)} %get-tuple-element.178, s32[1536]{0:T(1024)S(1)} %get-tuple-element.179, s32[512]{0:T(512)S(1)} %get-tuple-element.180, s32[1536]{0:T(1024)S(1)} %get-tuple-element.181, ...), kind=kLoop, calls=%fused_computation.9.clone.1 | loop fusion | flops 16515072 | bytes 3170304 | tf_op jit(solution)/shard_map/while/body/eval_jaxpr/convert_element_type | solution.py:26
  120.7 1.9 fusion.71
  123.6 13.6 %cosine_convert_fusion.2 = (bf16[512,1536]{1,0:T(8,128)(2,1)S(1)}, bf16[512,1536]{1,0:T(8,128)(2,1)S(1)}) fusion(s32[1536]{0:T(1024)S(1)} %get-tuple-element.177, s32[512]{0:T(512)S(1)} %get-tuple-element.178, s32[1536]{0:T(1024)S(1)} %get-tuple-element.179, s32[512]{0:T(512)S(1)} %get-tuple-element.180, s32[1536]{0:T(1024)S(1)} %get-tuple-element.181, ...), kind=kLoop, calls=%fused_computation.9.clone.1 | loop fusion | flops 16515072 | bytes 3170304 | tf_op jit(solution)/shard_map/while/body/eval_jaxpr/convert_element_type | solution.py:26
  137.2 1.8 fusion.71
  139.1 20.8 %copy.7 = bf16[2,8,512,1536]{3,2,1,0:T(8,128)(2,1)} copy(bf16[2,8,512,1536]{3,2,0,1:T(8,128)(2,1)} %bitcast.65) | data formatting | bytes 50331648 | tf_op jit(solution)/shard_map/transpose | solution.py:69
  159.9 12.3 %convolution_multiply_fusion.1 = f32[8192,64]{0,1:T(8,128)S(1)} fusion(bf16[8192,1536]{1,0:T(8,128)(2,1)} %bitcast.61, bf16[64,1536]{1,0:T(8,128)(2,1)S(1)} %copy-done), kind=kOutput, calls=%fused_computation.33 | convolution fusion | flops 1611137024 | bytes 27459584 | tf_op jit(solution)/shard_map/dot_general | solution.py:75
  174.0 6.0 %slice_bitcast_fusion = (bf16[256,2,64,64]{0,3,2,1:T(8,128)(2,1)}, bf16[256,2,64,64]{0,3,2,1:T(8,128)(2,1)}) fusion(bf16[2,256,2,64,64]{1,4,3,2,0:T(8,128)(2,1)} %param.11), kind=kLoop, calls=%fused_computation.50 | loop fusion | bytes 16777216 | tf_op jit(solution)/shard_map/squeeze | solution.py:82
  180.0 58.3 %reduce-scatter.3.cloned.1.call-done = f32[256,128]{0,1:T(8,128)} async-done(((f32[4096,128]{0,1:T(8,128)}), f32[256,128]{0,1:T(8,128)}) %reduce-scatter.3.cloned.1.call-update) | async-done | bytes 131088 | tf_op jit(solution)/shard_map/reduce_scatter | solution.py:81
  239.2 3.0 fusion.11
  243.7 36.9 %all-gather.3.cloned.1.call-done = bf16[4096,128]{1,0:T(8,128)(2,1)} async-done(((bf16[256,128]{1,0:T(8,128)(2,1)}), bf16[4096,128]{1,0:T(8,128)(2,1)}) %all-gather.3.cloned.1.call-update) | async-done | bytes 1048592 | tf_op jit(solution)/shard_map/all_gather | solution.py:83
  280.5 2.1 fusion.57
  282.6 10.1 %convolution_multiply_fusion.3 = f32[64,1536]{1,0:T(8,128)S(1)} fusion(bf16[8192,1536]{1,0:T(8,128)(2,1)} %bitcast.62, bf16[4096,64]{1,0:T(8,128)(2,1)S(1)} %get-tuple-element.135, bf16[4096,64]{1,0:T(8,128)(2,1)S(1)} %get-tuple-element.134), kind=kOutput, calls=%fused_computation.57 | convolution fusion | flops 1612808192 | bytes 26607616 | tf_op jit(solution)/shard_map/dot_general | solution.py:85
  293.8 12.3 %convolution_multiply_fusion = f32[8192,64]{0,1:T(8,128)S(1)} fusion(bf16[8192,1536]{1,0:T(8,128)(2,1)} %bitcast.63, bf16[64,1536]{1,0:T(8,128)(2,1)S(1)} %fusion.28), kind=kOutput, calls=%fused_computation.32 | convolution fusion | flops 1611137024 | bytes 27459584 | tf_op jit(solution)/shard_map/dot_general | solution.py:75
  306.3 1.5 pad_maximum_fusion.1
  307.8 60.6 %reduce-scatter.5.cloned.1.call-done = f32[256,128]{0,1:T(8,128)} async-done(((f32[4096,128]{0,1:T(8,128)}), f32[256,128]{0,1:T(8,128)}) %reduce-scatter.5.cloned.1.call-update) | async-done | bytes 131088 | tf_op jit(solution)/shard_map/reduce_scatter | solution.py:81
  369.3 3.0 fusion.15
  373.8 36.8 %all-gather.5.cloned.1.call-done = bf16[4096,128]{1,0:T(8,128)(2,1)} async-done(((bf16[256,128]{1,0:T(8,128)(2,1)}), bf16[4096,128]{1,0:T(8,128)(2,1)}) %all-gather.5.cloned.1.call-update) | async-done | bytes 1048592 | tf_op jit(solution)/shard_map/all_gather | solution.py:83
  410.6 2.1 fusion.56
  412.7 14.1 %fusion.31 = bf16[64,1536]{1,0:T(8,128)(2,1)} fusion(f32[64,1536]{1,0:T(8,128)S(1)} %convolution_bitcast_fusion, bf16[8192,1536]{1,0:T(8,128)(2,1)} %bitcast.64, bf16[4096,64]{1,0:T(8,128)(2,1)S(1)} %get-tuple-element.133, bf16[4096,64]{1,0:T(8,128)(2,1)S(1)} %get-tuple-element.132, f32[64]{0:T(128)S(1)} %get-tuple-element.140), kind=kOutput, calls=%fused_computation.78 | convolution fusion | flops 1619394560 | bytes 26804480 | tf_op jit(solution)/shard_map/dot_general | solution.py:85
  (61 shorter events, 15.6 us)
Async XLA Ops:
  6.5 153.4 %copy-start = (bf16[64,1536]{1,0:T(8,128)(2,1)S(1)}, bf16[64,1536]{1,0:T(8,128)(2,1)}, u32[]{:S(2)}) copy-start(bf16[64,1536]{1,0:T(8,128)(2,1)} %param.9) | copy-start | bytes 589828
  6.5 231.8 %reduce-scatter.3.cloned.1.call-start = ((), (), s32[]{:S(2)}) async-start(), calls=%async_computation.2 | async-start | bytes 2228224 | tf_op jit(solution)/shard_map/reduce_scatter | solution.py:81
  173.9 106.6 %all-gather.3.cloned.1.call-start = ((), (), s32[]{:S(2)}) async-start(), calls=%async_computation.3 | async-start | bytes 1114112 | tf_op jit(solution)/shard_map/all_gather | solution.py:83
  239.2 4.4 %copy-start.2 = (f32[2,64]{1,0:T(2,128)S(1)}, f32[2,64]{1,0:T(2,128)}, u32[]{:S(2)}) copy-start(f32[2,64]{1,0:T(2,128)} %param.13) | copy-start | bytes 1540
  243.4 125.1 %reduce-scatter.5.cloned.1.call-start = ((), (), s32[]{:S(2)}) async-start(), calls=%async_computation.4 | async-start | bytes 2228224 | tf_op jit(solution)/shard_map/reduce_scatter | solution.py:81
  282.6 10.1 %copy-start.1 = (bf16[2,64,64]{2,1,0:T(8,128)(2,1)S(1)}, bf16[2,64,64]{2,1,0:T(8,128)(2,1)}, u32[]{:S(2)}) copy-start(bf16[2,64,64]{2,1,0:T(8,128)(2,1)} %param.12) | copy-start | bytes 49156
  307.8 102.8 %all-gather.5.cloned.1.call-start = ((), (), s32[]{:S(2)}) async-start(), calls=%async_computation.5 | async-start | bytes 1114112 | tf_op jit(solution)/shard_map/all_gather | solution.py:83
Sparse Core Ops, SparseCore 0:
  174.0 64.2 reduce-scatter.2
  243.5 36.9 all-gather.2
  307.9 60.5 reduce-scatter.4
  373.7 36.8 all-gather.4
where the time goes:
time: 434 us; the launch traced here: 433 us
  waiting for transfers between devices  193 us (44%)
  other arithmetic  135 us (31%)
  matrix products  50.2 us (12%)
  local copies, waits for them, and re-layouts  41.8 us (10%)
  between operations  13.3 us (3%)
    reduce_scatter x2, waiting for transfers between devices, body(): lax.psum_scatter(partial_spectrum, 'pts', scatter_dimension=0, tiled=True)  119 us
    convert_element_type x8, other arithmetic, direct_basis(): jnp.cos(radians).astype(jnp.bfloat16)  109 us
    all_gather x2, waiting for transfers between devices, body(): gathered = lax.all_gather(mixed, 'pts', axis=0, tiled=True)  73.7 us
    dot_general x2, matrix products, body(): lax.dot_general(basis, current, (((1,), (1,)), ((), ())), preferred_eleme...  24.7 us
    dot_general x2, matrix products, body(): lax.dot_general(stacked, basis, (((0,), (0,)), ((), ())), preferred_eleme...  24.2 us
    transpose x1, local copies, waits for them, and re-layouts, body(): basis = blocked.reshape(block_count, 2, block_size, point_count).transpos...  20.8 us
    dynamic_update_slice x8, other arithmetic, body(): blocked = lax.map(basis_for, wave_blocks)  15.2 us
  transfers between devices with their start and end apart: 4, of which 4 were waited for; matrix products, arithmetic and copies ran while one was open for 1% of the time, Pallas kernels for 0%

commit v1 on v0

--- a/solution.py
+++ b/solution.py
@@ -80,7 +80,34 @@
         partial_spectrum = jnp.concatenate([product[:modes_total], product[modes_total:]], 1)
         spectrum = lax.psum_scatter(partial_spectrum, "pts", scatter_dimension=0, tiled=True)
         mixed = mix_modes(spectrum, spec_weight[depth])
-        gathered = lax.all_gather(mixed, "pts", axis=0, tiled=True)
+
+        def produce_layers_all_now(message, axis_name):
+            count_all = lax.axis_size(axis_name)
+            bank = []
+            jj = 0
+            while jj < count_all:
+                bank.append((jj, (jj + 1) % count_all))
+                jj = jj + 1
+            vals = []
+            jj = 0
+            while jj < count_all:
+                vals.append((jj, (jj - 1) % count_all))
+                jj = jj + 1
+            b_next, r1 = ([message], [message])
+            for _ in range(count_all // 2):
+                b_next.append(lax.ppermute(b_next[-1], axis_name, bank))
+            dev = 0
+            while dev < (count_all - 1) // 2:
+                r1.append(lax.ppermute(r1[-1], axis_name, vals))
+                dev = dev + 1
+            response = jnp.roll(
+                jnp.concatenate([*b_next[::-1], *r1[1:]], axis=0),
+                (lax.axis_index(axis_name) - count_all // 2) * message.shape[0],
+                axis=0,
+            )
+            return response
+
+        gathered = produce_layers_all_now(mixed, "pts")
         stacked = jnp.concatenate([gathered[:, :width], gathered[:, width:]], 0)
         spectral = lax.dot_general(
             stacked, basis, (((0,), (0,)), ((), ())), preferred_element_type=jnp.float32

time: 434 us -> 468 us (1.078)
  starting transfers between devices: 0.31 us -> 63.2 us
  waiting for transfers between devices: 193 us -> 160 us
  other arithmetic: 135 us -> 141 us
    all_gather x2 -> x0, waiting for transfers between devices: 73.7 us -> none  [body(): gathered = lax.all_gather(mixed, 'pts', axis=0, tiled=True)]
    ppermute x0 -> x30, starting transfers between devices: none -> 63.2 us  [the longest x14 63 us: produce_layers_all_now(): r1.append(lax.ppermute(r1[-1], axis_name, vals))]
    ppermute x0 -> x30, waiting for transfers between devices: none -> 39.2 us  [the longest x16 38.9 us: produce_layers_all_now(): b_next.append(lax.ppermute(b_next[-1], axis_name, bank))]
    concatenate x0 -> x2, other arithmetic: none -> 7.31 us  [produce_layers_all_now(): jnp.roll(jnp.concatenate([*b_next[::-1], *r1[1:]], axis=0), (lax.axis_ind...]
  transfers between devices with their start and end apart: 4 -> 32, of which waited for: 4 -> 19; matrix products, arithmetic and copies ran while one was open for 1% -> 1% of each run, Pallas kernels for 0% -> 0%
where the time goes in v1:
time: 468 us
  waiting for transfers between devices  160 us (34%)
  other arithmetic  141 us (30%)
  starting transfers between devices  63.2 us (14%)
  matrix products  50.2 us (11%)
  local copies, waits for them, and re-layouts  38.8 us (8%)
  between operations  13.8 us (3%)
    reduce_scatter x2, waiting for transfers between devices, body(): lax.psum_scatter(partial_spectrum, 'pts', scatter_dimension=0, tiled=True)  121 us
    convert_element_type x8, other arithmetic, direct_basis(): jnp.cos(radians).astype(jnp.bfloat16)  109 us
    ppermute x14, starting transfers between devices, produce_layers_all_now(): r1.append(lax.ppermute(r1[-1], axis_name, vals))  63 us
    ppermute x16, waiting for transfers between devices, produce_layers_all_now(): b_next.append(lax.ppermute(b_next[-1], axis_name, bank))  38.9 us
    dot_general x2, matrix products, body(): lax.dot_general(basis, current, (((1,), (1,)), ((), ())), preferred_eleme...  24.7 us
    dot_general x2, matrix products, body(): lax.dot_general(stacked, basis, (((0,), (0,)), ((), ())), preferred_eleme...  24.2 us
    transpose x1, local copies, waits for them, and re-layouts, body(): basis = blocked.reshape(block_count, 2, block_size, point_count).transpos...  20.8 us
    dynamic_update_slice x8, other arithmetic, body(): blocked = lax.map(basis_for, wave_blocks)  15.2 us
  transfers between devices with their start and end apart: 32, of which 19 were waited for; matrix products, arithmetic and copies ran while one was open for 1% of the time, Pallas kernels for 0%

profile of v1, /device:TPU:0, one launch (start us, length us, event | category | flops | bytes accessed | tf_op | source)
XLA Modules:
  0.0 467.5 jit_solution(4201541463412921354)
XLA Ops:
  7.3 131.7 %while.13 = (s32[]{:T(128)}, bf16[8,1024,1536]{2,1,0:T(8,128)(2,1)}, s32[8,512]{1,0:T(8,128)S(1)}, s32[3,1536]{1,0:T(4,128)}, s32[]{:T(128)}) while((s32[]{:T(128)}, bf16[8,1024,1536]{2,1,0:T(8,128)(2,1)}, s32[8,512]{1,0:T(8,128)S(1)}, s32[3,1536]{1,0:T(4,128)}, s32[]{:T(128)}) %tuple.58), condition=%wide.region_1.2_spmd, body=%wide.region_0.1_spmd.sunk | while | flops 22828544 | bytes 9511489 | solution.py:66
  8.2 13.6 %cosine_convert_fusion.2 = (bf16[512,1536]{1,0:T(8,128)(2,1)S(1)}, bf16[512,1536]{1,0:T(8,128)(2,1)S(1)}) fusion(s32[1536]{0:T(1024)S(1)} %get-tuple-element.178, s32[512]{0:T(512)S(1)} %get-tuple-element.179, s32[1536]{0:T(1024)S(1)} %get-tuple-element.180, s32[512]{0:T(512)S(1)} %get-tuple-element.181, s32[1536]{0:T(1024)S(1)} %get-tuple-element.182, ...), kind=kLoop, calls=%fused_computation.9.clone.1 | loop fusion | flops 16515072 | bytes 3170304 | tf_op jit(solution)/shard_map/while/body/eval_jaxpr/convert_element_type | solution.py:26
  24.7 13.6 %cosine_convert_fusion.2 = (bf16[512,1536]{1,0:T(8,128)(2,1)S(1)}, bf16[512,1536]{1,0:T(8,128)(2,1)S(1)}) fusion(s32[1536]{0:T(1024)S(1)} %get-tuple-element.178, s32[512]{0:T(512)S(1)} %get-tuple-element.179, s32[1536]{0:T(1024)S(1)} %get-tuple-element.180, s32[512]{0:T(512)S(1)} %get-tuple-element.181, s32[1536]{0:T(1024)S(1)} %get-tuple-element.182, ...), kind=kLoop, calls=%fused_computation.9.clone.1 | loop fusion | flops 16515072 | bytes 3170304 | tf_op jit(solution)/shard_map/while/body/eval_jaxpr/convert_element_type | solution.py:26
  41.2 13.6 %cosine_convert_fusion.2 = (bf16[512,1536]{1,0:T(8,128)(2,1)S(1)}, bf16[512,1536]{1,0:T(8,128)(2,1)S(1)}) fusion(s32[1536]{0:T(1024)S(1)} %get-tuple-element.178, s32[512]{0:T(512)S(1)} %get-tuple-element.179, s32[1536]{0:T(1024)S(1)} %get-tuple-element.180, s32[512]{0:T(512)S(1)} %get-tuple-element.181, s32[1536]{0:T(1024)S(1)} %get-tuple-element.182, ...), kind=kLoop, calls=%fused_computation.9.clone.1 | loop fusion | flops 16515072 | bytes 3170304 | tf_op jit(solution)/shard_map/while/body/eval_jaxpr/convert_element_type | solution.py:26
  57.6 13.6 %cosine_convert_fusion.2 = (bf16[512,1536]{1,0:T(8,128)(2,1)S(1)}, bf16[512,1536]{1,0:T(8,128)(2,1)S(1)}) fusion(s32[1536]{0:T(1024)S(1)} %get-tuple-element.178, s32[512]{0:T(512)S(1)} %get-tuple-element.179, s32[1536]{0:T(1024)S(1)} %get-tuple-element.180, s32[512]{0:T(512)S(1)} %get-tuple-element.181, s32[1536]{0:T(1024)S(1)} %get-tuple-element.182, ...), kind=kLoop, calls=%fused_computation.9.clone.1 | loop fusion | flops 16515072 | bytes 3170304 | tf_op jit(solution)/shard_map/while/body/eval_jaxpr/convert_element_type | solution.py:26
  74.2 13.6 %cosine_convert_fusion.2 = (bf16[512,1536]{1,0:T(8,128)(2,1)S(1)}, bf16[512,1536]{1,0:T(8,128)(2,1)S(1)}) fusion(s32[1536]{0:T(1024)S(1)} %get-tuple-element.178, s32[512]{0:T(512)S(1)} %get-tuple-element.179, s32[1536]{0:T(1024)S(1)} %get-tuple-element.180, s32[512]{0:T(512)S(1)} %get-tuple-element.181, s32[1536]{0:T(1024)S(1)} %get-tuple-element.182, ...), kind=kLoop, calls=%fused_computation.9.clone.1 | loop fusion | flops 16515072 | bytes 3170304 | tf_op jit(solution)/shard_map/while/body/eval_jaxpr/convert_element_type | solution.py:26
  90.6 13.6 %cosine_convert_fusion.2 = (bf16[512,1536]{1,0:T(8,128)(2,1)S(1)}, bf16[512,1536]{1,0:T(8,128)(2,1)S(1)}) fusion(s32[1536]{0:T(1024)S(1)} %get-tuple-element.178, s32[512]{0:T(512)S(1)} %get-tuple-element.179, s32[1536]{0:T(1024)S(1)} %get-tuple-element.180, s32[512]{0:T(512)S(1)} %get-tuple-element.181, s32[1536]{0:T(1024)S(1)} %get-tuple-element.182, ...), kind=kLoop, calls=%fused_computation.9.clone.1 | loop fusion | flops 16515072 | bytes 3170304 | tf_op jit(solution)/shard_map/while/body/eval_jaxpr/convert_element_type | solution.py:26
  107.0 13.6 %cosine_convert_fusion.2 = (bf16[512,1536]{1,0:T(8,128)(2,1)S(1)}, bf16[512,1536]{1,0:T(8,128)(2,1)S(1)}) fusion(s32[1536]{0:T(1024)S(1)} %get-tuple-element.178, s32[512]{0:T(512)S(1)} %get-tuple-element.179, s32[1536]{0:T(1024)S(1)} %get-tuple-element.180, s32[512]{0:T(512)S(1)} %get-tuple-element.181, s32[1536]{0:T(1024)S(1)} %get-tuple-element.182, ...), kind=kLoop, calls=%fused_computation.9.clone.1 | loop fusion | flops 16515072 | bytes 3170304 | tf_op jit(solution)/shard_map/while/body/eval_jaxpr/convert_element_type | solution.py:26
  123.6 13.6 %cosine_convert_fusion.2 = (bf16[512,1536]{1,0:T(8,128)(2,1)S(1)}, bf16[512,1536]{1,0:T(8,128)(2,1)S(1)}) fusion(s32[1536]{0:T(1024)S(1)} %get-tuple-element.178, s32[512]{0:T(512)S(1)} %get-tuple-element.179, s32[1536]{0:T(1024)S(1)} %get-tuple-element.180, s32[512]{0:T(512)S(1)} %get-tuple-element.181, s32[1536]{0:T(1024)S(1)} %get-tuple-element.182, ...), kind=kLoop, calls=%fused_computation.9.clone.1 | loop fusion | flops 16515072 | bytes 3170304 | tf_op jit(solution)/shard_map/while/body/eval_jaxpr/convert_element_type | solution.py:26
  139.0 20.8 %copy.7 = bf16[2,8,512,1536]{3,2,1,0:T(8,128)(2,1)} copy(bf16[2,8,512,1536]{3,2,0,1:T(8,128)(2,1)} %bitcast.65) | data formatting | bytes 50331648 | tf_op jit(solution)/shard_map/transpose | solution.py:69
  159.8 12.3 %convolution_multiply_fusion.1 = f32[8192,64]{0,1:T(8,128)S(1)} fusion(bf16[8192,1536]{1,0:T(8,128)(2,1)} %bitcast.61, bf16[64,1536]{1,0:T(8,128)(2,1)S(1)} %copy-done), kind=kOutput, calls=%fused_computation.33 | convolution fusion | flops 1611137024 | bytes 27459584 | tf_op jit(solution)/shard_map/dot_general | solution.py:75
  173.9 6.0 %slice_bitcast_fusion = (bf16[256,2,64,64]{0,3,2,1:T(8,128)(2,1)}, bf16[256,2,64,64]{0,3,2,1:T(8,128)(2,1)}) fusion(bf16[2,256,2,64,64]{1,4,3,2,0:T(8,128)(2,1)} %param.13), kind=kLoop, calls=%fused_computation.50 | loop fusion | bytes 16777216 | tf_op jit(solution)/shard_map/squeeze | solution.py:82
  179.9 58.3 %reduce-scatter.3.cloned.1.call-done = f32[256,128]{0,1:T(8,128)} async-done(((f32[4096,128]{0,1:T(8,128)}), f32[256,128]{0,1:T(8,128)}) %reduce-scatter.3.cloned.1.call-update) | async-done | bytes 131088 | tf_op jit(solution)/shard_map/reduce_scatter | solution.py:81
  242.7 6.4 %collective-permute-done = bf16[256,128]{1,0:T(8,128)(2,1)S(1)} collective-permute-done((bf16[256,128]{1,0:T(8,128)(2,1)S(1)}, bf16[256,128]{1,0:T(8,128)(2,1)S(1)}, u32[]{:S(2)}, u32[]{:S(2)}) %collective-permute-start) | collective-permute-done | bytes 65568 | tf_op jit(solution)/shard_map/ppermute | solution.py:98
  249.1 4.4 collective-permute-start.8
  255.6 4.4 collective-permute-start.9
  261.9 4.5 collective-permute-start.10
  268.4 4.5 collective-permute-start.11
  274.7 4.5 collective-permute-start.12
  281.1 4.5 collective-permute-start.13
  287.5 4.6 collective-permute-start.14
  298.3 10.1 %convolution_multiply_fusion.3 = f32[64,1536]{1,0:T(8,128)S(1)} fusion(bf16[8192,1536]{1,0:T(8,128)(2,1)} %bitcast.62, bf16[4096,64]{1,0:T(8,128)(2,1)S(1)} %get-tuple-element.136, bf16[4096,64]{1,0:T(8,128)(2,1)S(1)} %get-tuple-element.135), kind=kOutput, calls=%fused_computation.57 | convolution fusion | flops 1612808192 | bytes 26607616 | tf_op jit(solution)/shard_map/dot_general | solution.py:112
  309.5 12.3 %convolution_multiply_fusion = f32[8192,64]{0,1:T(8,128)S(1)} fusion(bf16[8192,1536]{1,0:T(8,128)(2,1)} %bitcast.63, bf16[64,1536]{1,0:T(8,128)(2,1)S(1)} %fusion.30), kind=kOutput, calls=%fused_computation.32 | convolution fusion | flops 1611137024 | bytes 27459584 | tf_op jit(solution)/shard_map/dot_general | solution.py:75
  323.5 62.8 %reduce-scatter.5.cloned.1.call-done = f32[256,128]{0,1:T(8,128)} async-done(((f32[4096,128]{0,1:T(8,128)}), f32[256,128]{0,1:T(8,128)}) %reduce-scatter.5.cloned.1.call-update) | async-done | bytes 131088 | tf_op jit(solution)/shard_map/reduce_scatter | solution.py:81
  390.8 6.4 %collective-permute-done.15 = bf16[256,128]{1,0:T(8,128)(2,1)S(1)} collective-permute-done((bf16[256,128]{1,0:T(8,128)(2,1)S(1)}, bf16[256,128]{1,0:T(8,128)(2,1)S(1)}, u32[]{:S(2)}, u32[]{:S(2)}) %collective-permute-start.15) | collective-permute-done | bytes 65568 | tf_op jit(solution)/shard_map/ppermute | solution.py:98
  403.6 4.4 collective-permute-start.24
  410.0 4.5 collective-permute-start.25
  416.4 4.5 collective-permute-start.26
  422.8 4.5 collective-permute-start.27
  429.2 4.5 collective-permute-start.28
  435.8 4.7 %collective-permute-start.29 = (bf16[256,128]{1,0:T(8,128)(2,1)S(1)}, bf16[256,128]{1,0:T(8,128)(2,1)S(1)}, u32[]{:S(2)}, u32[]{:S(2)}) collective-permute-start(bf16[256,128]{1,0:T(8,128)(2,1)S(1)} %collective-permute-done.28), channel_id=1, source_target_pairs={{0,15},{1,0},{2,1},{3,2},{4,3},{5,4},{6,5},{7,6},{8,7},{9,8},{10,9... | collective-permute-start | bytes 196616 | tf_op jit(solution)/shard_map/ppermute | solution.py:101
  446.5 14.1 %fusion.33 = bf16[64,1536]{1,0:T(8,128)(2,1)} fusion(f32[64,1536]{1,0:T(8,128)S(1)} %convolution_bitcast_fusion, bf16[8192,1536]{1,0:T(8,128)(2,1)} %bitcast.64, bf16[4096,64]{1,0:T(8,128)(2,1)S(1)} %get-tuple-element.134, bf16[4096,64]{1,0:T(8,128)(2,1)S(1)} %get-tuple-element.133, f32[64]{0:T(128)S(1)} %get-tuple-element.141), kind=kOutput, calls=%fused_computation.84 | convolution fusion | flops 1619394560 | bytes 26804480 | tf_op jit(solution)/shard_map/dot_general | solution.py:112
  (149 shorter events, 76.4 us)
Async XLA Ops:
  6.5 231.7 %reduce-scatter.3.cloned.1.call-start = ((), (), s32[]{:S(2)}) async-start(), calls=%async_computation.2 | async-start | bytes 2228224 | tf_op jit(solution)/shard_map/reduce_scatter | solution.py:81
  173.8 212.5 %reduce-scatter.5.cloned.1.call-start = ((), (), s32[]{:S(2)}) async-start(), calls=%async_computation.3 | async-start | bytes 2228224 | tf_op jit(solution)/shard_map/reduce_scatter | solution.py:81
  242.6 6.4 %collective-permute-start = (bf16[256,128]{1,0:T(8,128)(2,1)S(1)}, bf16[256,128]{1,0:T(8,128)(2,1)S(1)}, u32[]{:S(2)}, u32[]{:S(2)}) collective-permute-start(bf16[256,128]{1,0:T(8,128)(2,1)S(1)} %pad_maximum_fusion.2), channel_id=1, source_target_pairs={{0,1},{1,2},{2,3},{3,4},{4,5},{5,6},{6,7},{7,8},{8,9},{9,10},{10,1... | collective-permute-start | bytes 196616 | tf_op jit(solution)/shard_map/ppermute | solution.py:98
  249.1 6.5 %collective-permute-start.1 = (bf16[256,128]{1,0:T(8,128)(2,1)S(1)}, bf16[256,128]{1,0:T(8,128)(2,1)S(1)}, u32[]{:S(2)}, u32[]{:S(2)}) collective-permute-start(bf16[256,128]{1,0:T(8,128)(2,1)S(1)} %collective-permute-done), channel_id=1, source_target_pairs={{0,1},{1,2},{2,3},{3,4},{4,5},{5,6},{6,7},{7,8},{8,9},{9,10},{10,1... | collective-permute-start | bytes 196616 | tf_op jit(solution)/shard_map/ppermute | solution.py:98
  249.1 6.5 %collective-permute-start.8 = (bf16[256,128]{1,0:T(8,128)(2,1)S(1)}, bf16[256,128]{1,0:T(8,128)(2,1)S(1)}, u32[]{:S(2)}, u32[]{:S(2)}) collective-permute-start(bf16[256,128]{1,0:T(8,128)(2,1)S(1)} %pad_maximum_fusion.2), channel_id=1, source_target_pairs={{0,15},{1,0},{2,1},{3,2},{4,3},{5,4},{6,5},{7,6},{8,7},{9,8},{10,9... | collective-permute-start | bytes 196616 | tf_op jit(solution)/shard_map/ppermute | solution.py:101
  255.6 6.4 %collective-permute-start.2 = (bf16[256,128]{1,0:T(8,128)(2,1)S(1)}, bf16[256,128]{1,0:T(8,128)(2,1)S(1)}, u32[]{:S(2)}, u32[]{:S(2)}) collective-permute-start(bf16[256,128]{1,0:T(8,128)(2,1)S(1)} %collective-permute-done.1), channel_id=1, source_target_pairs={{0,1},{1,2},{2,3},{3,4},{4,5},{5,6},{6,7},{7,8},{8,9},{9,10},{10,1... | collective-permute-start | bytes 196616 | tf_op jit(solution)/shard_map/ppermute | solution.py:98
  255.6 6.4 %collective-permute-start.9 = (bf16[256,128]{1,0:T(8,128)(2,1)S(1)}, bf16[256,128]{1,0:T(8,128)(2,1)S(1)}, u32[]{:S(2)}, u32[]{:S(2)}) collective-permute-start(bf16[256,128]{1,0:T(8,128)(2,1)S(1)} %collective-permute-done.8), channel_id=1, source_target_pairs={{0,15},{1,0},{2,1},{3,2},{4,3},{5,4},{6,5},{7,6},{8,7},{9,8},{10,9... | collective-permute-start | bytes 196616 | tf_op jit(solution)/shard_map/ppermute | solution.py:101
  261.9 6.4 %collective-permute-start.3 = (bf16[256,128]{1,0:T(8,128)(2,1)S(1)}, bf16[256,128]{1,0:T(8,128)(2,1)S(1)}, u32[]{:S(2)}, u32[]{:S(2)}) collective-permute-start(bf16[256,128]{1,0:T(8,128)(2,1)S(1)} %collective-permute-done.2), channel_id=1, source_target_pairs={{0,1},{1,2},{2,3},{3,4},{4,5},{5,6},{6,7},{7,8},{8,9},{9,10},{10,1... | collective-permute-start | bytes 196616 | tf_op jit(solution)/shard_map/ppermute | solution.py:98
  261.9 6.4 %collective-permute-start.10 = (bf16[256,128]{1,0:T(8,128)(2,1)S(1)}, bf16[256,128]{1,0:T(8,128)(2,1)S(1)}, u32[]{:S(2)}, u32[]{:S(2)}) collective-permute-start(bf16[256,128]{1,0:T(8,128)(2,1)S(1)} %collective-permute-done.9), channel_id=1, source_target_pairs={{0,15},{1,0},{2,1},{3,2},{4,3},{5,4},{6,5},{7,6},{8,7},{9,8},{10,9... | collective-permute-start | bytes 196616 | tf_op jit(solution)/shard_map/ppermute | solution.py:101
  268.3 6.4 %collective-permute-start.4 = (bf16[256,128]{1,0:T(8,128)(2,1)S(1)}, bf16[256,128]{1,0:T(8,128)(2,1)S(1)}, u32[]{:S(2)}, u32[]{:S(2)}) collective-permute-start(bf16[256,128]{1,0:T(8,128)(2,1)S(1)} %collective-permute-done.3), channel_id=1, source_target_pairs={{0,1},{1,2},{2,3},{3,4},{4,5},{5,6},{6,7},{7,8},{8,9},{9,10},{10,1... | collective-permute-start | bytes 196616 | tf_op jit(solution)/shard_map/ppermute | solution.py:98
  268.4 6.4 %collective-permute-start.11 = (bf16[256,128]{1,0:T(8,128)(2,1)S(1)}, bf16[256,128]{1,0:T(8,128)(2,1)S(1)}, u32[]{:S(2)}, u32[]{:S(2)}) collective-permute-start(bf16[256,128]{1,0:T(8,128)(2,1)S(1)} %collective-permute-done.10), channel_id=1, source_target_pairs={{0,15},{1,0},{2,1},{3,2},{4,3},{5,4},{6,5},{7,6},{8,7},{9,8},{10,9... | collective-permute-start | bytes 196616 | tf_op jit(solution)/shard_map/ppermute | solution.py:101
  274.7 6.4 %collective-permute-start.5 = (bf16[256,128]{1,0:T(8,128)(2,1)S(1)}, bf16[256,128]{1,0:T(8,128)(2,1)S(1)}, u32[]{:S(2)}, u32[]{:S(2)}) collective-permute-start(bf16[256,128]{1,0:T(8,128)(2,1)S(1)} %collective-permute-done.4), channel_id=1, source_target_pairs={{0,1},{1,2},{2,3},{3,4},{4,5},{5,6},{6,7},{7,8},{8,9},{9,10},{10,1... | collective-permute-start | bytes 196616 | tf_op jit(solution)/shard_map/ppermute | solution.py:98
  274.7 6.4 %collective-permute-start.12 = (bf16[256,128]{1,0:T(8,128)(2,1)S(1)}, bf16[256,128]{1,0:T(8,128)(2,1)S(1)}, u32[]{:S(2)}, u32[]{:S(2)}) collective-permute-start(bf16[256,128]{1,0:T(8,128)(2,1)S(1)} %collective-permute-done.11), channel_id=1, source_target_pairs={{0,15},{1,0},{2,1},{3,2},{4,3},{5,4},{6,5},{7,6},{8,7},{9,8},{10,9... | collective-permute-start | bytes 196616 | tf_op jit(solution)/shard_map/ppermute | solution.py:101
  281.1 6.4 %collective-permute-start.6 = (bf16[256,128]{1,0:T(8,128)(2,1)S(1)}, bf16[256,128]{1,0:T(8,128)(2,1)S(1)}, u32[]{:S(2)}, u32[]{:S(2)}) collective-permute-start(bf16[256,128]{1,0:T(8,128)(2,1)S(1)} %collective-permute-done.5), channel_id=1, source_target_pairs={{0,1},{1,2},{2,3},{3,4},{4,5},{5,6},{6,7},{7,8},{8,9},{9,10},{10,1... | collective-permute-start | bytes 196616 | tf_op jit(solution)/shard_map/ppermute | solution.py:98
  281.1 6.4 %collective-permute-start.13 = (bf16[256,128]{1,0:T(8,128)(2,1)S(1)}, bf16[256,128]{1,0:T(8,128)(2,1)S(1)}, u32[]{:S(2)}, u32[]{:S(2)}) collective-permute-start(bf16[256,128]{1,0:T(8,128)(2,1)S(1)} %collective-permute-done.12), channel_id=1, source_target_pairs={{0,15},{1,0},{2,1},{3,2},{4,3},{5,4},{6,5},{7,6},{8,7},{9,8},{10,9... | collective-permute-start | bytes 196616 | tf_op jit(solution)/shard_map/ppermute | solution.py:101
  287.5 6.4 %collective-permute-start.7 = (bf16[256,128]{1,0:T(8,128)(2,1)S(1)}, bf16[256,128]{1,0:T(8,128)(2,1)S(1)}, u32[]{:S(2)}, u32[]{:S(2)}) collective-permute-start(bf16[256,128]{1,0:T(8,128)(2,1)S(1)} %collective-permute-done.6), channel_id=1, source_target_pairs={{0,1},{1,2},{2,3},{3,4},{4,5},{5,6},{6,7},{7,8},{8,9},{9,10},{10,1... | collective-permute-start | bytes 196616 | tf_op jit(solution)/shard_map/ppermute | solution.py:98
  287.5 6.7 %collective-permute-start.14 = (bf16[256,128]{1,0:T(8,128)(2,1)S(1)}, bf16[256,128]{1,0:T(8,128)(2,1)S(1)}, u32[]{:S(2)}, u32[]{:S(2)}) collective-permute-start(bf16[256,128]{1,0:T(8,128)(2,1)S(1)} %collective-permute-done.13), channel_id=1, source_target_pairs={{0,15},{1,0},{2,1},{3,2},{4,3},{5,4},{6,5},{7,6},{8,7},{9,8},{10,9... | collective-permute-start | bytes 196616 | tf_op jit(solution)/shard_map/ppermute | solution.py:101
  390.7 6.4 %collective-permute-start.15 = (bf16[256,128]{1,0:T(8,128)(2,1)S(1)}, bf16[256,128]{1,0:T(8,128)(2,1)S(1)}, u32[]{:S(2)}, u32[]{:S(2)}) collective-permute-start(bf16[256,128]{1,0:T(8,128)(2,1)S(1)} %pad_maximum_fusion.3), channel_id=1, source_target_pairs={{0,1},{1,2},{2,3},{3,4},{4,5},{5,6},{6,7},{7,8},{8,9},{9,10},{10,1... | collective-permute-start | bytes 196616 | tf_op jit(solution)/shard_map/ppermute | solution.py:98
  397.1 6.5 %collective-permute-start.16 = (bf16[256,128]{1,0:T(8,128)(2,1)S(1)}, bf16[256,128]{1,0:T(8,128)(2,1)S(1)}, u32[]{:S(2)}, u32[]{:S(2)}) collective-permute-start(bf16[256,128]{1,0:T(8,128)(2,1)S(1)} %collective-permute-done.15), channel_id=1, source_target_pairs={{0,1},{1,2},{2,3},{3,4},{4,5},{5,6},{6,7},{7,8},{8,9},{9,10},{10,1... | collective-permute-start | bytes 196616 | tf_op jit(solution)/shard_map/ppermute | solution.py:98
  397.2 6.5 %collective-permute-start.23 = (bf16[256,128]{1,0:T(8,128)(2,1)S(1)}, bf16[256,128]{1,0:T(8,128)(2,1)S(1)}, u32[]{:S(2)}, u32[]{:S(2)}) collective-permute-start(bf16[256,128]{1,0:T(8,128)(2,1)S(1)} %pad_maximum_fusion.3), channel_id=1, source_target_pairs={{0,15},{1,0},{2,1},{3,2},{4,3},{5,4},{6,5},{7,6},{8,7},{9,8},{10,9... | collective-permute-start | bytes 196616 | tf_op jit(solution)/shard_map/ppermute | solution.py:101
  403.6 6.4 %collective-permute-start.17 = (bf16[256,128]{1,0:T(8,128)(2,1)S(1)}, bf16[256,128]{1,0:T(8,128)(2,1)S(1)}, u32[]{:S(2)}, u32[]{:S(2)}) collective-permute-start(bf16[256,128]{1,0:T(8,128)(2,1)S(1)} %collective-permute-done.16), channel_id=1, source_target_pairs={{0,1},{1,2},{2,3},{3,4},{4,5},{5,6},{6,7},{7,8},{8,9},{9,10},{10,1... | collective-permute-start | bytes 196616 | tf_op jit(solution)/shard_map/ppermute | solution.py:98
  403.6 6.4 %collective-permute-start.24 = (bf16[256,128]{1,0:T(8,128)(2,1)S(1)}, bf16[256,128]{1,0:T(8,128)(2,1)S(1)}, u32[]{:S(2)}, u32[]{:S(2)}) collective-permute-start(bf16[256,128]{1,0:T(8,128)(2,1)S(1)} %collective-permute-done.23), channel_id=1, source_target_pairs={{0,15},{1,0},{2,1},{3,2},{4,3},{5,4},{6,5},{7,6},{8,7},{9,8},{10,9... | collective-permute-start | bytes 196616 | tf_op jit(solution)/shard_map/ppermute | solution.py:101
  410.0 6.4 %collective-permute-start.18 = (bf16[256,128]{1,0:T(8,128)(2,1)S(1)}, bf16[256,128]{1,0:T(8,128)(2,1)S(1)}, u32[]{:S(2)}, u32[]{:S(2)}) collective-permute-start(bf16[256,128]{1,0:T(8,128)(2,1)S(1)} %collective-permute-done.17), channel_id=1, source_target_pairs={{0,1},{1,2},{2,3},{3,4},{4,5},{5,6},{6,7},{7,8},{8,9},{9,10},{10,1... | collective-permute-start | bytes 196616 | tf_op jit(solution)/shard_map/ppermute | solution.py:98
  410.0 6.4 %collective-permute-start.25 = (bf16[256,128]{1,0:T(8,128)(2,1)S(1)}, bf16[256,128]{1,0:T(8,128)(2,1)S(1)}, u32[]{:S(2)}, u32[]{:S(2)}) collective-permute-start(bf16[256,128]{1,0:T(8,128)(2,1)S(1)} %collective-permute-done.24), channel_id=1, source_target_pairs={{0,15},{1,0},{2,1},{3,2},{4,3},{5,4},{6,5},{7,6},{8,7},{9,8},{10,9... | collective-permute-start | bytes 196616 | tf_op jit(solution)/shard_map/ppermute | solution.py:101
  416.4 6.4 %collective-permute-start.19 = (bf16[256,128]{1,0:T(8,128)(2,1)S(1)}, bf16[256,128]{1,0:T(8,128)(2,1)S(1)}, u32[]{:S(2)}, u32[]{:S(2)}) collective-permute-start(bf16[256,128]{1,0:T(8,128)(2,1)S(1)} %collective-permute-done.18), channel_id=1, source_target_pairs={{0,1},{1,2},{2,3},{3,4},{4,5},{5,6},{6,7},{7,8},{8,9},{9,10},{10,1... | collective-permute-start | bytes 196616 | tf_op jit(solution)/shard_map/ppermute | solution.py:98
  416.4 6.4 %collective-permute-start.26 = (bf16[256,128]{1,0:T(8,128)(2,1)S(1)}, bf16[256,128]{1,0:T(8,128)(2,1)S(1)}, u32[]{:S(2)}, u32[]{:S(2)}) collective-permute-start(bf16[256,128]{1,0:T(8,128)(2,1)S(1)} %collective-permute-done.25), channel_id=1, source_target_pairs={{0,15},{1,0},{2,1},{3,2},{4,3},{5,4},{6,5},{7,6},{8,7},{9,8},{10,9... | collective-permute-start | bytes 196616 | tf_op jit(solution)/shard_map/ppermute | solution.py:101
  422.8 6.4 %collective-permute-start.20 = (bf16[256,128]{1,0:T(8,128)(2,1)S(1)}, bf16[256,128]{1,0:T(8,128)(2,1)S(1)}, u32[]{:S(2)}, u32[]{:S(2)}) collective-permute-start(bf16[256,128]{1,0:T(8,128)(2,1)S(1)} %collective-permute-done.19), channel_id=1, source_target_pairs={{0,1},{1,2},{2,3},{3,4},{4,5},{5,6},{6,7},{7,8},{8,9},{9,10},{10,1... | collective-permute-start | bytes 196616 | tf_op jit(solution)/shard_map/ppermute | solution.py:98
  422.8 6.4 %collective-permute-start.27 = (bf16[256,128]{1,0:T(8,128)(2,1)S(1)}, bf16[256,128]{1,0:T(8,128)(2,1)S(1)}, u32[]{:S(2)}, u32[]{:S(2)}) collective-permute-start(bf16[256,128]{1,0:T(8,128)(2,1)S(1)} %collective-permute-done.26), channel_id=1, source_target_pairs={{0,15},{1,0},{2,1},{3,2},{4,3},{5,4},{6,5},{7,6},{8,7},{9,8},{10,9... | collective-permute-start | bytes 196616 | tf_op jit(solution)/shard_map/ppermute | solution.py:101
  429.2 6.4 %collective-permute-start.21 = (bf16[256,128]{1,0:T(8,128)(2,1)S(1)}, bf16[256,128]{1,0:T(8,128)(2,1)S(1)}, u32[]{:S(2)}, u32[]{:S(2)}) collective-permute-start(bf16[256,128]{1,0:T(8,128)(2,1)S(1)} %collective-permute-done.20), channel_id=1, source_target_pairs={{0,1},{1,2},{2,3},{3,4},{4,5},{5,6},{6,7},{7,8},{8,9},{9,10},{10,1... | collective-permute-start | bytes 196616 | tf_op jit(solution)/shard_map/ppermute | solution.py:98
  429.2 6.6 %collective-permute-start.28 = (bf16[256,128]{1,0:T(8,128)(2,1)S(1)}, bf16[256,128]{1,0:T(8,128)(2,1)S(1)}, u32[]{:S(2)}, u32[]{:S(2)}) collective-permute-start(bf16[256,128]{1,0:T(8,128)(2,1)S(1)} %collective-permute-done.27), channel_id=1, source_target_pairs={{0,15},{1,0},{2,1},{3,2},{4,3},{5,4},{6,5},{7,6},{8,7},{9,8},{10,9... | collective-permute-start | bytes 196616 | tf_op jit(solution)/shard_map/ppermute | solution.py:101
  435.6 6.4 %collective-permute-start.22 = (bf16[256,128]{1,0:T(8,128)(2,1)S(1)}, bf16[256,128]{1,0:T(8,128)(2,1)S(1)}, u32[]{:S(2)}, u32[]{:S(2)}) collective-permute-start(bf16[256,128]{1,0:T(8,128)(2,1)S(1)} %collective-permute-done.21), channel_id=1, source_target_pairs={{0,1},{1,2},{2,3},{3,4},{4,5},{5,6},{6,7},{7,8},{8,9},{9,10},{10,1... | collective-permute-start | bytes 196616 | tf_op jit(solution)/shard_map/ppermute | solution.py:98
  435.8 6.6 %collective-permute-start.29 = (bf16[256,128]{1,0:T(8,128)(2,1)S(1)}, bf16[256,128]{1,0:T(8,128)(2,1)S(1)}, u32[]{:S(2)}, u32[]{:S(2)}) collective-permute-start(bf16[256,128]{1,0:T(8,128)(2,1)S(1)} %collective-permute-done.28), channel_id=1, source_target_pairs={{0,15},{1,0},{2,1},{3,2},{4,3},{5,4},{6,5},{7,6},{8,7},{9,8},{10,9... | collective-permute-start | bytes 196616 | tf_op jit(solution)/shard_map/ppermute | solution.py:101
  (3 other events, 211.8 us)
Sparse Core Ops, SparseCore 0:
  173.9 64.2 reduce-scatter.2
  323.6 62.6 reduce-scatter.4
